TPU v7x, 32 devices: a whole 2x2x4 slice. The times are simulated.
32 devices in a mesh: freq: 4 (over z), src: 8 (over y, x, core).
Axes of the slice: x: 2, y: 2, z: 4, core: 2. Of those that a mesh axis runs over, the one named last changes fastest.
Arguments:
- jones: bfloat16 [1, 128, 8, 128, 1024], P(None, None, None, 'freq', 'src'), may hold values from -3 to 3
- directions: float32 [1, 3, 1024], P(None, None, 'src'), may hold values from -1 to 1
- brightness: float32 [1024], P('src'), may hold values from 0.1 to 4
- spectral: float32 [1024], P('src'), may hold values from 0 to 2.5
- antennas: float32 [3, 128], replicated, may hold values from -50 to 50
- visible: int32 [1, 512], replicated, may hold values from 0 to 1023, as said below
- pairs: int32 [2, 256], replicated, may hold values from 0 to 127, as said below
- group_of: int32 [256], replicated, may hold values from 0 to 63, as said below
Outputs:
- spectra: float32 [64, 1, 4, 128], P(('freq', 'src'))
Inputs may be any that keep to these rules, and one draw needn't show every extreme that they name: `visible`: each row is sorted ascending without repeats. Its entries lie in a cyclic run of 640 consecutive catalog positions whose middle 512 - 512 // 4 positions are all present; for sidereal time 0 that run passes from 1023 to 0. pairs[0, n] < pairs[1, n]; no antenna pair repeats. `group_of`: never falls along the baselines; every group has a baseline. The groups of device d (in the order freq, src) are d * 2 to d * 2 + 1; their baselines number 2 to 14, exactly 14 on some device.
All inputs are finite; a program needn't handle non-finite values.
Results may differ from a plain program's by a relative error of at most 0.0032.
Values may be sent and summed in bfloat16 or wider, within the bound.
A program may use at most 64 MiB of HBM per device.

v0:
```python
import math

import jax
import jax.numpy as jnp
from jax import lax
from jax.sharding import PartitionSpec as P

BD = 8
GD = 2


SPEED_LIGHT = 299792458.0
START_FREQ = 100000000.0
BAND_WIDTH = 100000000.0
PIVOT_FREQ = 150000000.0
HIGHEST = lax.Precision.HIGHEST


def channel_freq(channel, chan_count):
    return START_FREQ + channel.astype(jnp.float32) * (BAND_WIDTH / chan_count)


def geometry(antennas, directions):
    return (
        antennas[0][:, None] * directions[0][None, :]
        + antennas[1][:, None] * directions[1][None, :]
        + antennas[2][:, None] * directions[2][None, :]
    )


def channel_matrix(beam, geo_term, brightness, spectral, weight, frequency):
    phases = 2.0 * math.pi / SPEED_LIGHT * frequency * geo_term
    cos_grid = jnp.cos(phases)[:, None, None, :]
    sin_grid = jnp.sin(phases)[:, None, None, :]
    amplitude = jnp.sqrt(brightness * jnp.exp(-spectral * jnp.log(frequency / PIVOT_FREQ))) * weight
    antenna_total = beam.shape[0]
    beam_float = beam.astype(jnp.float32)
    beam_real = beam_float[:, 0:4].reshape(antenna_total, 2, 2, -1)
    beam_imag = beam_float[:, 4:8].reshape(antenna_total, 2, 2, -1)
    z_real = (
        (amplitude * (beam_real * cos_grid + beam_imag * sin_grid))
        .reshape(2 * antenna_total, -1)
        .astype(jnp.bfloat16)
    )
    z_imag = (
        (amplitude * (beam_imag * cos_grid - beam_real * sin_grid))
        .reshape(2 * antenna_total, -1)
        .astype(jnp.bfloat16)
    )
    left_side = jnp.concatenate([z_real, z_imag], axis=1)
    right_side = jnp.concatenate([left_side, jnp.concatenate([-z_imag, z_real], axis=1)], axis=0)
    return lax.dot_general(
        left_side, right_side, (((1,), (1,)), ((), ())), preferred_element_type=jnp.float32
    )


def selection_index(first_antenna, second_antenna, antenna_total):
    component = jnp.arange(8, dtype=jnp.int32)
    partition_indices = component // 4
    left_polarization = component % 4 // 2
    right_polarization = component % 2
    row_indices = first_antenna[None, :] * 2 + left_polarization[:, None]
    column_indices = (
        partition_indices[:, None] * (2 * antenna_total)
        + second_antenna[None, :] * 2
        + right_polarization[:, None]
    )
    return row_indices * (4 * antenna_total) + column_indices


def delay_tables(chan_count):
    chan_ids = jnp.arange(chan_count, dtype=jnp.int32)
    angles = 2.0 * math.pi / chan_count * chan_ids.astype(jnp.float32)
    taper = (
        0.35875
        - 0.48829 * jnp.cos(angles)
        + 0.14128 * jnp.cos(2.0 * angles)
        - 0.01168 * jnp.cos(3.0 * angles)
    )
    wrapped = chan_ids[:, None] * chan_ids[None, :] % chan_count
    phases = 2.0 * math.pi / chan_count * wrapped.astype(jnp.float32)
    return (jnp.cos(phases) * taper[None, :], jnp.sin(phases) * taper[None, :])


def delay_power(vis_data):
    cos_table, sin_table = delay_tables(vis_data.shape[0])
    vis_real = vis_data[:, :, 0:4]
    vis_imag = vis_data[:, :, 4:8]
    pattern = "uk,ktpb->utpb"
    delay_real = jnp.einsum(pattern, cos_table, vis_real, precision=HIGHEST) + jnp.einsum(
        pattern, sin_table, vis_imag, precision=HIGHEST
    )
    delay_imag = jnp.einsum(pattern, cos_table, vis_imag, precision=HIGHEST) - jnp.einsum(
        pattern, sin_table, vis_real, precision=HIGHEST
    )
    return delay_real * delay_real + delay_imag * delay_imag


def per_device(jones, directions, brightness, spectral, antennas, visible, pairs, group_of):
    antenna_total = jones.shape[1]
    chan_dev = jones.shape[3]
    freq_devices = lax.axis_size("freq")
    src_devices = lax.axis_size("src")
    devices = freq_devices * src_devices
    chan_count = chan_dev * freq_devices
    rows_each = chan_dev // src_devices
    vis_total = visible.shape[1]
    device_id = lax.axis_index("freq") * src_devices + lax.axis_index("src")
    chan_base = lax.axis_index("freq") * chan_dev
    owner_ids = jnp.arange(devices, dtype=jnp.int32)
    slot_cap = 2 * BD - GD
    owner_of = group_of // GD
    owner_loads = jnp.sum((owner_of[None, :] == owner_ids[:, None]).astype(jnp.int32), axis=1)
    owner_first = jnp.cumsum(owner_loads) - owner_loads
    offsets = jnp.arange(slot_cap, dtype=jnp.int32)
    baseline = owner_first[:, None] + offsets[None, :]
    slot_live = offsets[None, :] < owner_loads[:, None]
    baseline = jnp.where(slot_live, baseline, 0)
    flat_base = baseline.reshape(-1)
    live_weight = slot_live.reshape(-1).astype(jnp.float32)
    pick_flat = selection_index(pairs[0][flat_base], pairs[1][flat_base], antenna_total)

    def slot_values(beam, geo_term, bright, slopes, weight, frequency):
        matrix = channel_matrix(beam, geo_term, bright, slopes, weight, frequency)
        return matrix.reshape(-1)[pick_flat] * live_weight[None, :]

    source_rows = jnp.concatenate([directions, jnp.stack([brightness, spectral])[None]], axis=1)
    beams_all = lax.all_to_all(jones, "src", split_axis=3, concat_axis=4, tiled=True)
    table_all = lax.all_gather(source_rows, "src", axis=2, tiled=True)
    sub_base = chan_base + lax.axis_index("src") * rows_each
    selected = []
    chosen = visible[0]
    beam_sel = jnp.take(beams_all[0], chosen, axis=3)
    table_sel = jnp.take(table_all[0], chosen, axis=1)
    selected.append((beam_sel, geometry(antennas, table_sel[0:3]), table_sel[3], table_sel[4]))
    unit_weight = jnp.ones((vis_total,), jnp.float32)

    def own_terms(channel):
        frequency = channel_freq(sub_base + channel, chan_count)
        return jnp.stack(
            [
                slot_values(
                    lax.dynamic_index_in_dim(entry[0], channel, 2, keepdims=False),
                    entry[1],
                    entry[2],
                    entry[3],
                    unit_weight,
                    frequency,
                )
                for entry in selected
            ]
        )

    summed = lax.map(own_terms, jnp.arange(rows_each, dtype=jnp.int32))
    owned_vis = lax.all_to_all(summed, ("freq", "src"), split_axis=3, concat_axis=0, tiled=True)
    power_slots = delay_power(owned_vis)
    local_base = lax.dynamic_index_in_dim(baseline, device_id, 0, keepdims=False)
    local_live = lax.dynamic_index_in_dim(
        slot_live.astype(jnp.float32), device_id, 0, keepdims=False
    )
    local_groups = group_of[local_base]
    my_groups = device_id * GD + jnp.arange(GD, dtype=jnp.int32)
    counts = jnp.sum((group_of[None, :] == my_groups[:, None]).astype(jnp.float32), axis=1)
    member = (local_groups[:, None] == my_groups[None, :]).astype(jnp.float32) * local_live[:, None]
    totals = jnp.einsum("utpb,bg->gtpu", power_slots, member, precision=HIGHEST)
    return totals / (counts[:, None, None, None] * (vis_total * chan_count))


def solution(mesh):
    return jax.shard_map(
        per_device,
        mesh=mesh,
        in_specs=(
            P(None, None, None, "freq", "src"),
            P(None, None, "src"),
            P("src"),
            P("src"),
            P(),
            P(),
            P(),
            P(),
        ),
        out_specs=P(("freq", "src"), None, None, None),
        check_vma=False,
    )
```

profile of v0, /device:TPU:0, one launch (start us, length us, event | category | flops | bytes accessed | tf_op | source)
XLA Modules:
  0.0 310.5 jit_solution(4252532293105092048)
XLA Ops:
  0.0 9.8 %copy.37 = bf16[1,128,8,32,128]{4,2,1,0,3:T(8,128)(2,1)} copy(bf16[1,128,8,32,128]{4,3,2,1,0:T(8,128)(2,1)} %param.10) | data formatting | bytes 16777216 | tf_op args[0]
  9.8 5.3 %all-to-all-start = ((bf16[1,128,8,32,128]{4,2,1,0,3:T(8,128)(2,1)}), bf16[1,128,8,32,128]{4,2,1,0,3:T(8,128)(2,1)}, u32[]{:S(2)}, u32[]{:S(2)}) async-start(bf16[1,128,8,32,128]{4,2,1,0,3:T(8,128)(2,1)} %copy.37), calls=%async_computation | async-start | bytes 16777216 | tf_op jit(solution)/shard_map/all_to_all | solution.py:128
  15.9 3.2 %gather_fusion.4 = s32[448]{0:T(512)S(1)} fusion(s32[256]{0:T(256)S(1)} %bitcast.117, s32[1024]{0:T(1024)S(1)} %pad_clamp_fusion.1), kind=kCustom, calls=%fused_computation.4 | custom fusion | bytes 5376 | tf_op jit(solution)/shard_map/gather | solution.py:121
  19.0 3.2 %gather_fusion.5 = s32[448]{0:T(512)S(1)} fusion(s32[256]{0:T(256)S(1)} %bitcast.116, s32[1024]{0:T(1024)S(1)} %pad_clamp_fusion.1), kind=kCustom, calls=%fused_computation.5 | custom fusion | bytes 5376 | tf_op jit(solution)/shard_map/gather | solution.py:121
  23.3 90.6 %all_gather.3 = f32[1,5,1024]{1,2,0:T(8,128)S(1)} all-gather(f32[1,5,128]{1,2,0:T(8,128)S(1)} %pad_maximum_fusion), channel_id=1, replica_groups=mesh['freq'=4,'src'=8] {'src'}, dimensions={2}, use_global_device_ids=true | all-gather | bytes 23040 | tf_op jit(solution)/shard_map/all_gather | solution.py:129
  116.2 13.3 %copy.38 = bf16[1,128,8,8,4,128]{1,2,4,5,3,0:T(8,128)(2,1)} copy(bf16[1,128,8,8,4,128]{5,2,1,4,3,0:T(8,128)(2,1)} %bitcast.14) | data formatting | bytes 16777216 | tf_op jit(solution)/shard_map/all_to_all | solution.py:128
  129.5 6.5 %gather_fusion.3 = bf16[512,128,8,4]{1,2,3,0:T(8,128)(2,1)} fusion(bf16[128,8,4,1024]{0,1,2,3:T(8,128)(2,1)} %bitcast.125, s32[1024]{0:T(1024)S(1)} %pad_clamp_fusion.2), kind=kCustom, calls=%fused_computation.3 | custom fusion | bytes 8390656 | tf_op jit(solution)/shard_map/jit(_take)/gather | solution.py:133
  136.1 4.5 %select_bitcast_fusion = bf16[128,8,4,512]{0,1,2,3:T(8,128)(2,1)} fusion(bf16[512,128,8,4]{1,2,3,0:T(8,128)(2,1)} %gather_fusion.3, pred[512]{0:T(512)(128)(4,1)S(1)} %compare_and_fusion), kind=kLoop, calls=%fused_computation.37 | loop fusion | flops 2097152 | bytes 8389120 | tf_op jit(solution)/shard_map/jit(_take)/select_n | solution.py:133
  140.6 143.1 %while.13 = (s32[]{:T(128)}, f32[4,1,8,448]{3,2,1,0:T(8,128)S(1)}, s32[4]{0:T(128)S(1)}, s32[]{:T(128)}, f32[1,1,1,512]{3,2,1,0:T(1,128)S(1)}, /*index=5*/f32[51...) while((s32[]{:T(128)}, f32[4,1,8,448]{3,2,1,0:T(8,128)S(1)}, ...), condition=%wide.region_3.4_spmd.clone, body=%wide.region_2.3_spmd.clone.sunk | while | flops 551196032 | bytes 44794732 | solution.py:154
  144.3 2.5 copy.64
  153.9 1.8 fusion.97
  157.2 18.9 %gather_fusion = f32[3584]{0:T(1024)S(1)} fusion(f32[131072]{0:T(1024)S(1)} %bitcast.115, s32[4096]{0:T(1024)S(1)} %pad_clamp_fusion.5), kind=kCustom, calls=%fused_computation.clone.clone.1 | custom fusion | bytes 43008 | tf_op jit(solution)/shard_map/while/body/eval_jaxpr/gather | solution.py:125
  180.1 2.5 copy.64
  189.7 1.8 fusion.97
  193.0 18.9 %gather_fusion = f32[3584]{0:T(1024)S(1)} fusion(f32[131072]{0:T(1024)S(1)} %bitcast.115, s32[4096]{0:T(1024)S(1)} %pad_clamp_fusion.5), kind=kCustom, calls=%fused_computation.clone.clone.1 | custom fusion | bytes 43008 | tf_op jit(solution)/shard_map/while/body/eval_jaxpr/gather | solution.py:125
  215.8 2.5 copy.64
  225.5 1.8 fusion.97
  228.8 18.9 %gather_fusion = f32[3584]{0:T(1024)S(1)} fusion(f32[131072]{0:T(1024)S(1)} %bitcast.115, s32[4096]{0:T(1024)S(1)} %pad_clamp_fusion.5), kind=kCustom, calls=%fused_computation.clone.clone.1 | custom fusion | bytes 43008 | tf_op jit(solution)/shard_map/while/body/eval_jaxpr/gather | solution.py:125
  251.6 2.5 copy.64
  261.2 1.8 fusion.97
  264.6 18.9 %gather_fusion = f32[3584]{0:T(1024)S(1)} fusion(f32[131072]{0:T(1024)S(1)} %bitcast.115, s32[4096]{0:T(1024)S(1)} %pad_clamp_fusion.5), kind=kCustom, calls=%fused_computation.clone.clone.1 | custom fusion | bytes 43008 | tf_op jit(solution)/shard_map/while/body/eval_jaxpr/gather | solution.py:125
  285.5 3.8 %reduce.11 = f32[448,4,8]{2,1,0:T(4,128)S(1)} reduce(f32[448,4,1,8]{3,2,1,0:T(1,128)S(1)} %bitcast.126, f32[]{:T(128)} %broadcast.435), dimensions={2}, to_apply=%bitcast.87.reduce_sub_computation | reduce | bytes 114692
  290.8 5.7 %all-to-all-start.1 = ((f32[32,1,448]{2,1,0:T(1,128)}), f32[32,1,448]{2,1,0:T(1,128)S(1)}, u32[]{:S(2)}, u32[]{:S(2)}) async-start(f32[32,1,448]{2,1,0:T(1,128)} %reshape.467), calls=%async_computation.1 | async-start | bytes 131072 | tf_op jit(solution)/shard_map/all_to_all | solution.py:155
  296.5 7.4 %all-to-all-done.1 = f32[32,1,448]{2,1,0:T(1,128)S(1)} async-done(((f32[32,1,448]{2,1,0:T(1,128)}), f32[32,1,448]{2,1,0:T(1,128)S(1)}, u32[]{:S(2)}, u32[]{:S(2)}) %all-to-all-start.1) | async-done | bytes 57376 | tf_op jit(solution)/shard_map/all_to_all | solution.py:155
  (175 shorter events, 54.0 us)
Async XLA Ops:
  9.8 5.4 %copy-start = (s32[256]{0:T(256)S(1)}, s32[256]{0:T(256)}, u32[]{:S(2)}) copy-start(s32[256]{0:T(256)} %param.17) | copy-start | bytes 3076
  9.8 6.0 %copy-start.3 = (s32[2,256]{1,0:T(2,128)S(1)}, s32[2,256]{1,0:T(2,128)}, u32[]{:S(2)}) copy-start(s32[2,256]{1,0:T(2,128)} %param.16) | copy-start | bytes 6148
  9.8 106.4 %all-to-all-start = ((bf16[1,128,8,32,128]{4,2,1,0,3:T(8,128)(2,1)}), bf16[1,128,8,32,128]{4,2,1,0,3:T(8,128)(2,1)}, u32[]{:S(2)}, u32[]{:S(2)}) async-start(bf16[1,128,8,32,128]{4,2,1,0,3:T(8,128)(2,1)} %copy.37), calls=%async_computation | async-start | bytes 16777216 | tf_op jit(solution)/shard_map/all_to_all | solution.py:128
  15.1 7.1 %copy-start.6 = (f32[128]{0:T(128)S(1)}, f32[128]{0:T(128)}, u32[]{:S(2)}) copy-start(f32[128]{0:T(128)} %param.13) | copy-start | bytes 1540
  15.1 7.1 %copy-start.7 = (f32[128]{0:T(128)S(1)}, f32[128]{0:T(128)}, u32[]{:S(2)}) copy-start(f32[128]{0:T(128)} %param.12) | copy-start | bytes 1540
  15.2 7.2 %copy-start.4 = (f32[1,3,128]{2,0,1:T(1,128)S(1)}, f32[1,3,128]{2,0,1:T(1,128)}, u32[]{:S(2)}) copy-start(f32[1,3,128]{2,0,1:T(1,128)} %param.11) | copy-start | bytes 4612
  15.2 98.7 %copy-start.2 = (s32[1,512]{1,0:T(1,128)S(1)}, s32[1,512]{1,0:T(1,128)}, u32[]{:S(2)}) copy-start(s32[1,512]{1,0:T(1,128)} %param.15) | copy-start | bytes 6148
  15.2 101.0 %copy-start.5 = (f32[3,128]{1,0:T(4,128)S(1)}, f32[3,128]{1,0:T(4,128)}, u32[]{:S(2)}) copy-start(f32[3,128]{1,0:T(4,128)} %param.14) | copy-start | bytes 4612
  153.8 1.9 copy-start.1
  189.6 1.9 copy-start.1
  225.4 1.9 copy-start.1
  261.2 1.9 copy-start.1
  290.8 13.1 %all-to-all-start.1 = ((f32[32,1,448]{2,1,0:T(1,128)}), f32[32,1,448]{2,1,0:T(1,128)S(1)}, u32[]{:S(2)}, u32[]{:S(2)}) async-start(f32[32,1,448]{2,1,0:T(1,128)} %reshape.467), calls=%async_computation.1 | async-start | bytes 131072 | tf_op jit(solution)/shard_map/all_to_all | solution.py:155
where the time goes:
time: 312 us; the launch traced here: 310 us
  local copies, waits for them, and re-layouts  155 us (50%)
  blocking collectives  90.6 us (29%)
  other arithmetic  30.4 us (10%)
  starting transfers between devices  11 us (4%)
  loops' own time  10.1 us (3%)
  waiting for transfers between devices  7.39 us (2%)
  matrix products  5.14 us (2%)
    all_gather x1, blocking collectives, per_device(): table_all = lax.all_gather(source_rows, 'src', axis=2, tiled=True)  90.6 us
    gather x8, local copies, waits for them, and re-layouts, slot_values(): return matrix.reshape(-1)[pick_flat] * live_weight[None, :]  75.7 us
    while x36, local copies, waits for them, and re-layouts  23.3 us
    unnamed x21, local copies, waits for them, and re-layouts  13.6 us
    all_to_all x1, local copies, waits for them, and re-layouts, per_device(): lax.all_to_all(jones, 'src', split_axis=3, concat_axis=4, tiled=True)  13.3 us
    another operation x1, loops' own time, per_device(): summed = lax.map(own_terms, jnp.arange(rows_each, dtype=jnp.int32))  10.1 us
    all_to_all x1, waiting for transfers between devices, per_device(): lax.all_to_all(summed, ('freq', 'src'), split_axis=3, concat_axis=0, tile...  7.39 us
    neg x4, other arithmetic, channel_matrix(): -z_imag  7.19 us
  transfers between devices with their start and end apart: 2, of which 1 were waited for; matrix products, arithmetic and copies ran while one was open for 3% of the time, Pallas kernels for 0%

commit v1 on v0

v1 whole, which is shorter than its diff:
```python
import functools
import math

import jax
import jax.numpy as jnp
import numpy as np
from jax import lax
from jax.experimental import pallas as pl
from jax.experimental.pallas import tpu as pltpu
from jax.sharding import PartitionSpec as P

GD = 2
SLOTS = 16
SPEED_LIGHT = 299792458.0
START_FREQ = 100000000.0
BAND_WIDTH = 100000000.0
PIVOT_FREQ = 150000000.0
HIGHEST = lax.Precision.HIGHEST
F32 = jnp.float32
BF16 = jnp.bfloat16
MESH = pl.DeviceIdType.MESH
ABLK = 16

SIN_C = [(-1.0) ** i / math.factorial(2 * i + 1) for i in range(6)]
COS_C = [(-1.0) ** i / math.factorial(2 * i) for i in range(7)]


def dot_t(a, b):
    return lax.dot_general(a, b, (((1,), (1,)), ((), ())), preferred_element_type=F32)


def cos_sin_turns(x):
    r = x - jnp.round(x)
    h = r * math.pi
    h2 = h * h
    s = SIN_C[-1]
    for c in SIN_C[-2::-1]:
        s = s * h2 + c
    s = s * h
    c_ = COS_C[-1]
    for c in COS_C[-2::-1]:
        c_ = c_ * h2 + c
    s2 = s + s
    return 1.0 - s2 * s, s2 * c_


def vis_kernel(
    nf, ns, chan_count,
    jones_ref, dir_ref, bright_ref, spec_ref, ant_ref, visible_ref, pairs_ref, group_ref,
    out_ref,
    zbuf, geo_ref, stepc_ref, steps_ref, amp_ref, oa_ref, ob_ref, vbuf,
):
    step = pl.program_id(0)
    steps = pl.num_programs(0)
    na = ant_ref.shape[1]
    kd = jones_ref.shape[3]
    sd = jones_ref.shape[4]
    nbl = pairs_ref.shape[1]
    vis_total = visible_ref.shape[1]
    df = BAND_WIDTH / chan_count
    chan_base = lax.axis_index("freq") * kd

    @pl.when(step == 0)
    def _():
        ants = jnp.transpose(
            jnp.concatenate([ant_ref[...], jnp.zeros((na - 3, na), F32)], axis=0)
        )
        dirs = dir_ref[0]
        geo = (
            ants[:, 0:1] * dirs[0:1, :]
            + ants[:, 1:2] * dirs[1:2, :]
            + ants[:, 2:3] * dirs[2:3, :]
        )
        geo_ref[...] = geo
        c8, s8 = cos_sin_turns(geo * (8.0 * df / SPEED_LIGHT))
        stepc_ref[...] = c8
        steps_ref[...] = s8
        at = lax.broadcasted_iota(jnp.int32, (sd, vis_total), 0) + lax.axis_index("src") * sd
        hit = (at == visible_ref[...]).astype(F32).astype(BF16)
        weight = dot_t(jnp.ones((8, vis_total), BF16), hit)[0:1]
        chan = lax.broadcasted_iota(jnp.int32, (kd, sd), 0) + chan_base
        freq = START_FREQ + chan.astype(F32) * df
        amp_ref[...] = (
            jnp.sqrt(bright_ref[...] * jnp.exp(-spec_ref[...] * jnp.log(freq / PIVOT_FREQ)))
            * weight
        )
        ids = lax.broadcasted_iota(jnp.int32, (na, nbl), 0)
        oa_ref[...] = (ids == pairs_ref[0:1, :]).astype(F32).astype(BF16)
        ob_ref[...] = (ids == pairs_ref[1:2, :]).astype(F32)

    chan8 = lax.broadcasted_iota(jnp.int32, (8, sd), 0) + chan_base
    turn_rate = (START_FREQ + chan8.astype(F32) * df) * (1.0 / SPEED_LIGHT)

    def build(i, carry):
        a = step * ABLK + i
        c, s = cos_sin_turns(geo_ref[pl.ds(a, 1), :] * turn_rate)
        cd = stepc_ref[pl.ds(a, 1), :]
        sdl = steps_ref[pl.ds(a, 1), :]
        cs, ss = [c], [s]
        for _ in range(kd // 8 - 1):
            c, s = c * cd - s * sdl, s * cd + c * sdl
            cs.append(c)
            ss.append(s)
        amp = amp_ref[...]
        ca = jnp.concatenate(cs, axis=0) * amp
        sa = jnp.concatenate(ss, axis=0) * amp
        rows = pl.ds(pl.multiple_of(a * kd, kd), kd)
        for pq in range(4):
            br = jones_ref[0, i, pq].astype(F32)
            bi = jones_ref[0, i, 4 + pq].astype(F32)
            zbuf[pq, rows, :] = br * ca + bi * sa
            zbuf[4 + pq, rows, :] = bi * ca - br * sa
        return carry

    lax.fori_loop(0, ABLK, build, 0, unroll=4)

    @pl.when(step == steps - 1)
    def _():
        def channel(k, carry):
            def z(r, p, q):
                return zbuf[4 * r + 2 * p + q, pl.ds(k, na, stride=kd), :].astype(BF16)

            zr = jnp.concatenate(
                [jnp.concatenate([z(0, p, 0), z(0, p, 1)], axis=1) for p in range(2)], axis=0
            )
            zi = jnp.concatenate(
                [jnp.concatenate([z(1, p, 0), z(1, p, 1)], axis=1) for p in range(2)], axis=0
            )
            left = jnp.concatenate([zr, zi], axis=1)
            turned = jnp.concatenate([zi, -zr], axis=1)
            oa = oa_ref[...]
            ob = ob_ref[...]
            rows = []
            for right in (left, turned):
                gram = dot_t(left, right).astype(BF16)
                for p in range(2):
                    picked = jnp.dot(
                        gram[:, p * na : (p + 1) * na], oa, preferred_element_type=F32
                    )
                    for p2 in range(2):
                        rows.append(
                            jnp.sum(
                                picked[p2 * na : (p2 + 1) * na] * ob, axis=0, keepdims=True
                            )
                        )
            vis = jnp.concatenate(rows, axis=0)
            for t in range(nbl // 128):
                vbuf[t, pl.ds(k, 8, stride=kd), :] = vis[:, t * 128 : (t + 1) * 128]
            return carry

        lax.fori_loop(0, kd, channel, 0)
        owner = group_ref[...] // GD
        devices = nf * ns
        mine = lax.broadcasted_iota(jnp.int32, (devices, nbl), 0) == owner
        mine_f = mine.astype(F32)
        before = lax.broadcasted_iota(jnp.int32, (nbl, nbl), 0) < lax.broadcasted_iota(
            jnp.int32, (nbl, nbl), 1
        )
        counts = jnp.dot(
            mine_f.astype(BF16), before.astype(F32).astype(BF16), preferred_element_type=F32
        )
        rank = jnp.sum(counts * mine_f, axis=0, keepdims=True).astype(jnp.int32)
        slot = ((owner % ns) * nf + owner // ns) * SLOTS + rank
        vals = jnp.concatenate([vbuf[t] for t in range(nbl // 128)], axis=1).astype(BF16)
        per = nf * SLOTS
        for j in range(ns):
            place = lax.broadcasted_iota(jnp.int32, (per, nbl), 0) + j * per
            hit = (place == slot).astype(F32).astype(BF16)
            out_ref[j] = dot_t(hit, vals).astype(BF16)


def local_vis(nf, ns, chan_count, jones, directions, bright, spec, antennas, visible, pairs, groups):
    na, kd, sd = jones.shape[1], jones.shape[3], jones.shape[4]
    nbl = pairs.shape[1]
    whole = lambda x: pl.BlockSpec(x.shape, lambda i: (0,) * x.ndim)
    small = (directions, bright, spec, antennas, visible, pairs, groups)
    out = jax.ShapeDtypeStruct((ns, nf * SLOTS, 8 * kd), BF16)
    return pl.pallas_call(
        functools.partial(vis_kernel, nf, ns, chan_count),
        grid=(na // ABLK,),
        out_shape=out,
        in_specs=[pl.BlockSpec((1, ABLK, 8, kd, sd), lambda i: (0, i, 0, 0, 0))]
        + [whole(x) for x in small],
        out_specs=pl.BlockSpec(out.shape, lambda i: (0, 0, 0)),
        scratch_shapes=[
            pltpu.VMEM((8, na * kd, sd), F32),
            pltpu.VMEM((na, sd), F32),
            pltpu.VMEM((na, sd), F32),
            pltpu.VMEM((na, sd), F32),
            pltpu.VMEM((kd, sd), F32),
            pltpu.VMEM((na, nbl), BF16),
            pltpu.VMEM((na, nbl), F32),
            pltpu.VMEM((nbl // 128, 8 * kd, 128), F32),
        ],
        compiler_params=pltpu.CompilerParams(vmem_limit_bytes=48 * 1024 * 1024),
    )(jones, *small)


def exchange_kernel(
    nf, ns, scale, w_ref, table_ref, group_ref, out_ref,
    rbuf, sbuf, zbuf, send1, recv1, send2, recv2,
):
    f = lax.axis_index("freq")
    j = lax.axis_index("src")
    kd = w_ref.shape[2] // 8

    barrier = pltpu.get_barrier_semaphore()
    for o in range(1, ns):
        pl.semaphore_signal(
            barrier, inc=1, device_id=(f, lax.rem(j + o, ns)), device_id_type=MESH
        )
    for o in range(1, nf):
        pl.semaphore_signal(
            barrier, inc=1, device_id=(lax.rem(f + o, nf), j), device_id_type=MESH
        )
    pl.semaphore_wait(barrier, ns + nf - 2)

    first = []
    for o in range(1, ns):
        to = lax.rem(j + o, ns)
        copy = pltpu.make_async_remote_copy(
            src_ref=w_ref.at[to],
            dst_ref=rbuf.at[o - 1],
            send_sem=send1.at[o - 1],
            recv_sem=recv1.at[o - 1],
            device_id=(f, to),
            device_id_type=MESH,
        )
        copy.start()
        first.append(copy)
    total = w_ref[j].astype(F32)
    for o in range(1, ns):
        first[o - 1].wait_recv()
        total = total + rbuf[o - 1].astype(F32)
    sbuf[...] = total.reshape(nf, SLOTS, 8 * kd)

    second = []
    for o in range(1, nf):
        to = lax.rem(f + o, nf)
        copy = pltpu.make_async_remote_copy(
            src_ref=sbuf.at[to],
            dst_ref=zbuf.at[f],
            send_sem=send2.at[o - 1],
            recv_sem=recv2.at[o - 1],
            device_id=(to, j),
            device_id_type=MESH,
        )
        copy.start()
        second.append(copy)
    zbuf[f] = sbuf[f]
    dev = f * ns + j
    groups = group_ref[...]
    shape = (8, 4 * SLOTS)
    row = lax.broadcasted_iota(jnp.int32, shape, 0)
    col = lax.broadcasted_iota(jnp.int32, shape, 1)
    mean = jnp.zeros(shape, F32)
    start = jnp.zeros((1, 1), F32)
    slot = (col % SLOTS).astype(F32)
    for g in range(GD):
        count = jnp.sum((groups == dev * GD + g).astype(F32), axis=1, keepdims=True)
        inside = (row // 4 == g) & (row % 4 == col // SLOTS)
        inside = inside & (slot >= start) & (slot < start + count)
        mean = mean + jnp.where(inside, 1.0 / (count * scale), 0.0)
        start = start + count
    for copy in second:
        copy.wait_recv()
    blocks = [zbuf[i] for i in range(nf)]
    vis = jnp.concatenate(
        [
            jnp.concatenate([b[:, c * kd : (c + 1) * kd] for b in blocks], axis=1)
            for c in range(8)
        ],
        axis=0,
    )
    both = jnp.dot(vis, table_ref[...], precision=HIGHEST, preferred_element_type=F32)
    nu = table_ref.shape[1] // 2
    half = 4 * SLOTS
    real = both[:half, :nu] + both[half:, nu:]
    imag = both[half:, :nu] - both[:half, nu:]
    power = real * real + imag * imag
    out_ref[...] = jnp.dot(mean, power, precision=HIGHEST, preferred_element_type=F32)
    for copy in first + second:
        copy.wait_send()


def exchange(nf, ns, scale, w, table, groups):
    kd = w.shape[2] // 8
    vmem = pl.BlockSpec(memory_space=pltpu.VMEM)
    return pl.pallas_call(
        functools.partial(exchange_kernel, nf, ns, scale),
        out_shape=jax.ShapeDtypeStruct((8, table.shape[1] // 2), F32),
        in_specs=[vmem] * 3,
        out_specs=vmem,
        scratch_shapes=[
            pltpu.VMEM((ns - 1, nf * SLOTS, 8 * kd), BF16),
            pltpu.VMEM((nf, SLOTS, 8 * kd), F32),
            pltpu.VMEM((nf, SLOTS, 8 * kd), F32),
            pltpu.SemaphoreType.DMA((ns - 1,)),
            pltpu.SemaphoreType.DMA((ns - 1,)),
            pltpu.SemaphoreType.DMA((nf - 1,)),
            pltpu.SemaphoreType.DMA((nf - 1,)),
        ],
        compiler_params=pltpu.CompilerParams(
            collective_id=0, has_side_effects=True, vmem_limit_bytes=16 * 1024 * 1024
        ),
    )(w, table, groups)


def delay_table(chan_count):
    k = np.arange(chan_count)
    angles = 2.0 * np.pi * k / chan_count
    taper = (
        0.35875
        - 0.48829 * np.cos(angles)
        + 0.14128 * np.cos(2.0 * angles)
        - 0.01168 * np.cos(3.0 * angles)
    )
    phases = 2.0 * np.pi * ((k[:, None] * k[None, :]) % chan_count) / chan_count
    both = np.concatenate([np.cos(phases), np.sin(phases)], axis=1) * taper[:, None]
    return both.astype(np.float32)


def per_device(nf, ns, jones, directions, brightness, spectral, antennas, visible, pairs, group_of):
    chan_count = jones.shape[3] * nf
    groups = group_of.reshape(1, -1)
    w = local_vis(
        nf, ns, chan_count, jones, directions, brightness.reshape(1, -1),
        spectral.reshape(1, -1), antennas, visible, pairs, groups,
    )
    table = jnp.asarray(delay_table(chan_count))
    out = exchange(nf, ns, float(visible.shape[1] * chan_count), w, table, groups)
    return out.reshape(GD, 1, 4, chan_count)


def solution(mesh):
    nf, ns = mesh.shape["freq"], mesh.shape["src"]
    return jax.shard_map(
        functools.partial(per_device, nf, ns),
        mesh=mesh,
        in_specs=(
            P(None, None, None, "freq", "src"),
            P(None, None, "src"),
            P("src"),
            P("src"),
            P(),
            P(),
            P(),
            P(),
        ),
        out_specs=P(("freq", "src"), None, None, None),
        check_vma=False,
    )
```

time: 312 us -> 67.8 us (0.22)
  local copies, waits for them, and re-layouts: 155 us -> 5.35 us
  blocking collectives: 90.6 us -> 0 us
  Pallas kernels: 0 us -> 62.1 us
  other arithmetic: 30.4 us -> 0 us
  starting transfers between devices: 11 us -> 0 us
  loops' own time: 10.1 us -> 0 us
  waiting for transfers between devices: 7.39 us -> 0 us
  matrix products: 5.14 us -> 0 us
    all_gather x1 -> x0, blocking collectives: 90.6 us -> none  [per_device(): table_all = lax.all_gather(source_rows, 'src', axis=2, tiled=True)]
    gather x13 -> x0, local copies, waits for them, and re-layouts: 90.3 us -> none  [the longest x8 75.7 us: slot_values(): return matrix.reshape(-1)[pick_flat] * live_weight[None, :]]
    pallas_call x0 -> x2, Pallas kernels: none -> 62.1 us  [the longest x1 48.1 us: local_vis(): pl.pallas_call(functools.partial(vis_kernel, nf, ns, chan_count), grid=(n...]
    while x37 -> x0, local copies, waits for them, and re-layouts: 24.5 us -> none
    all_to_all x3 -> x0, local copies, waits for them, and re-layouts: 14.5 us -> none  [the longest x1 13.3 us: per_device(): lax.all_to_all(jones, 'src', split_axis=3, concat_axis=4, tiled=True)]
    all_to_all x2 -> x0, starting transfers between devices: 11 us -> none  [the longest x1 5.71 us: per_device(): lax.all_to_all(summed, ('freq', 'src'), split_axis=3, concat_axis=0, tile...]
    another operation x1 -> x0, loops' own time: 10.1 us -> none  [per_device(): summed = lax.map(own_terms, jnp.arange(rows_each, dtype=jnp.int32))]
    unnamed x21 -> x16, local copies, waits for them, and re-layouts: 13.6 us -> 5.35 us
  transfers between devices with their start and end apart: 2 -> 0, of which waited for: 1 -> 0; matrix products, arithmetic and copies ran while one was open for 3% -> 0% of each run, Pallas kernels for 0% -> 0%
where the time goes in v1:
time: 67.8 us; the launch traced here: 67.4 us
  Pallas kernels  62.1 us (92%)
  local copies, waits for them, and re-layouts  5.35 us (8%)
    pallas_call x1, Pallas kernels, local_vis(): pl.pallas_call(functools.partial(vis_kernel, nf, ns, chan_count), grid=(n...  48.1 us
    pallas_call x1, Pallas kernels, exchange(): pl.pallas_call(functools.partial(exchange_kernel, nf, ns, scale), out_sha...  14 us
    unnamed x16, local copies, waits for them, and re-layouts  5.35 us

profile of v1, /device:TPU:0, one launch (start us, length us, event | category | flops | bytes accessed | tf_op | source)
XLA Modules:
  0.0 67.4 jit_solution(6884189855502614469)
XLA Ops:
  0.0 0.0 copy-start
  0.0 0.7 %copy.10.dir_ref = f32[1,3,128]{2,1,0:T(4,128)S(1)} copy(f32[1,3,128]{2,0,1:T(1,128)} %param.10) | data formatting | bytes 3072 | tf_op args[1]
  0.7 0.0 copy-start.1
  0.7 0.7 %copy-done.1 = s32[256]{0:T(256)S(1)} copy-done((s32[256]{0:T(256)S(1)}, s32[256]{0:T(256)}, u32[]{:S(2)}) %copy-start.1) | copy-done | bytes 1048
  1.4 0.0 copy-start.2
  1.4 0.7 %copy-done.2 = f32[3,128]{1,0:T(4,128)S(1)} copy-done((f32[3,128]{1,0:T(4,128)S(1)}, f32[3,128]{1,0:T(4,128)}, u32[]{:S(2)}) %copy-start.2) | copy-done | bytes 1560
  2.1 0.0 copy-start.3
  2.1 0.7 %copy-done.3 = s32[1,512]{1,0:T(1,128)S(1)} copy-done((s32[1,512]{1,0:T(1,128)S(1)}, s32[1,512]{1,0:T(1,128)}, u32[]{:S(2)}) %copy-start.3) | copy-done | bytes 2072
  2.8 0.0 copy-start.4
  2.8 0.7 %copy-done.4 = s32[2,256]{1,0:T(2,128)S(1)} copy-done((s32[2,256]{1,0:T(2,128)S(1)}, s32[2,256]{1,0:T(2,128)}, u32[]{:S(2)}) %copy-start.4) | copy-done | bytes 2072
  3.4 0.0 copy-start.5
  3.4 0.7 copy-done.5
  4.1 0.0 copy-start.6
  4.1 0.7 copy-done.6
  4.8 48.1 %shard_map.91.w_ref = bf16[8,64,256]{2,1,0:T(8,128)(2,1)S(1)} custom-call(bf16[1,128,8,32,128]{4,3,2,1,0:T(8,128)(2,1)} %jones_ref.1, f32[1,3,128]{2,1,0:T(4,128)S(1)} %copy.10.dir_ref, f32[1,128]{1,0:T(1,128)S(1)} %bitcast.9, f32[1,128]{1,0:T(1,128)S(1)} %bitcast.10, f32[3,128]{1,0:T(4,128)S(1)} %copy-done.2, s32[1,512]{1,0:T(1,128)S(1)} %copy-done.3, ...), custom_call_target="tpu_custom_call" | custom-call | tf_op jit(solution)/shard_map/pallas_call | solution.py:178
  52.9 0.0 copy-done
  52.9 14.0 %shard_map.92 = f32[8,128]{1,0:T(8,128)S(1)} custom-call(bf16[8,64,256]{2,1,0:T(8,128)(2,1)S(1)} %shard_map.91.w_ref, f32[128,256]{1,0:T(8,128)S(1)} %copy-done, s32[1,256]{1,0:T(1,128)S(1)} %bitcast.8), custom_call_target="tpu_custom_call" | custom-call | tf_op jit(solution)/shard_map/pallas_call | solution.py:289
  66.9 0.6 copy.13
Async XLA Ops:
  0.0 52.9 %copy-start = (f32[128,256]{1,0:T(8,128)S(1)}, f32[128,256]{1,0:T(8,128)}, u32[]{:S(2)}) copy-start(f32[128,256]{1,0:T(8,128)} %constant.2.clone.table_ref) | copy-start | bytes 393220
  0.7 0.7 %copy-start.1 = (s32[256]{0:T(256)S(1)}, s32[256]{0:T(256)}, u32[]{:S(2)}) copy-start(s32[256]{0:T(256)} %param.16) | copy-start | bytes 3076
  1.4 0.7 %copy-start.2 = (f32[3,128]{1,0:T(4,128)S(1)}, f32[3,128]{1,0:T(4,128)}, u32[]{:S(2)}) copy-start(f32[3,128]{1,0:T(4,128)} %ant_ref.1) | copy-start | bytes 4612
  2.1 0.7 %copy-start.3 = (s32[1,512]{1,0:T(1,128)S(1)}, s32[1,512]{1,0:T(1,128)}, u32[]{:S(2)}) copy-start(s32[1,512]{1,0:T(1,128)} %visible_ref.1) | copy-start | bytes 6148
  2.8 0.7 %copy-start.4 = (s32[2,256]{1,0:T(2,128)S(1)}, s32[2,256]{1,0:T(2,128)}, u32[]{:S(2)}) copy-start(s32[2,256]{1,0:T(2,128)} %pairs_ref.1) | copy-start | bytes 6148
  3.4 0.7 copy-start.5
  4.1 0.7 copy-start.6

commit v2 on v1

--- a/solution.py
+++ b/solution.py
@@ -20,6 +20,7 @@
 BF16 = jnp.bfloat16
 MESH = pl.DeviceIdType.MESH
 ABLK = 16
+PAD = 8
 
 SIN_C = [(-1.0) ** i / math.factorial(2 * i + 1) for i in range(6)]
 COS_C = [(-1.0) ** i / math.factorial(2 * i) for i in range(7)]
@@ -104,7 +105,7 @@
         amp = amp_ref[...]
         ca = jnp.concatenate(cs, axis=0) * amp
         sa = jnp.concatenate(ss, axis=0) * amp
-        rows = pl.ds(pl.multiple_of(a * kd, kd), kd)
+        rows = pl.ds(pl.multiple_of(a * (kd + PAD), 8), kd)
         for pq in range(4):
             br = jones_ref[0, i, pq].astype(F32)
             bi = jones_ref[0, i, 4 + pq].astype(F32)
@@ -118,7 +119,7 @@
     def _():
         def channel(k, carry):
             def z(r, p, q):
-                return zbuf[4 * r + 2 * p + q, pl.ds(k, na, stride=kd), :].astype(BF16)
+                return zbuf[4 * r + 2 * p + q, pl.ds(k, na, stride=kd + PAD), :].astype(BF16)
 
             zr = jnp.concatenate(
                 [jnp.concatenate([z(0, p, 0), z(0, p, 1)], axis=1) for p in range(2)], axis=0
@@ -148,7 +149,7 @@
                 vbuf[t, pl.ds(k, 8, stride=kd), :] = vis[:, t * 128 : (t + 1) * 128]
             return carry
 
-        lax.fori_loop(0, kd, channel, 0)
+        lax.fori_loop(0, kd, channel, 0, unroll=8)
         owner = group_ref[...] // GD
         devices = nf * ns
         mine = lax.broadcasted_iota(jnp.int32, (devices, nbl), 0) == owner
@@ -183,7 +184,7 @@
         + [whole(x) for x in small],
         out_specs=pl.BlockSpec(out.shape, lambda i: (0, 0, 0)),
         scratch_shapes=[
-            pltpu.VMEM((8, na * kd, sd), F32),
+            pltpu.VMEM((8, na * (kd + PAD), sd), F32),
             pltpu.VMEM((na, sd), F32),
             pltpu.VMEM((na, sd), F32),
             pltpu.VMEM((na, sd), F32),
@@ -192,7 +193,7 @@
             pltpu.VMEM((na, nbl), F32),
             pltpu.VMEM((nbl // 128, 8 * kd, 128), F32),
         ],
-        compiler_params=pltpu.CompilerParams(vmem_limit_bytes=48 * 1024 * 1024),
+        compiler_params=pltpu.CompilerParams(vmem_limit_bytes=60 * 1024 * 1024),
     )(jones, *small)
 
 
@@ -228,26 +229,6 @@
         )
         copy.start()
         first.append(copy)
-    total = w_ref[j].astype(F32)
-    for o in range(1, ns):
-        first[o - 1].wait_recv()
-        total = total + rbuf[o - 1].astype(F32)
-    sbuf[...] = total.reshape(nf, SLOTS, 8 * kd)
-
-    second = []
-    for o in range(1, nf):
-        to = lax.rem(f + o, nf)
-        copy = pltpu.make_async_remote_copy(
-            src_ref=sbuf.at[to],
-            dst_ref=zbuf.at[f],
-            send_sem=send2.at[o - 1],
-            recv_sem=recv2.at[o - 1],
-            device_id=(to, j),
-            device_id_type=MESH,
-        )
-        copy.start()
-        second.append(copy)
-    zbuf[f] = sbuf[f]
     dev = f * ns + j
     groups = group_ref[...]
     shape = (8, 4 * SLOTS)
@@ -262,6 +243,26 @@
         inside = inside & (slot >= start) & (slot < start + count)
         mean = mean + jnp.where(inside, 1.0 / (count * scale), 0.0)
         start = start + count
+    total = w_ref[j].astype(F32)
+    for o in range(1, ns):
+        first[o - 1].wait_recv()
+        total = total + rbuf[o - 1].astype(F32)
+    sbuf[...] = total.reshape(nf, SLOTS, 8 * kd)
+
+    second = []
+    for o in range(1, nf):
+        to = lax.rem(f + o, nf)
+        copy = pltpu.make_async_remote_copy(
+            src_ref=sbuf.at[to],
+            dst_ref=zbuf.at[f],
+            send_sem=send2.at[o - 1],
+            recv_sem=recv2.at[o - 1],
+            device_id=(to, j),
+            device_id_type=MESH,
+        )
+        copy.start()
+        second.append(copy)
+    zbuf[f] = sbuf[f]
     for copy in second:
         copy.wait_recv()
     blocks = [zbuf[i] for i in range(nf)]

time: 67.8 us -> 38.3 us (0.56)
  Pallas kernels: 62.1 us -> 35.2 us
  local copies, waits for them, and re-layouts: 5.35 us -> 2.84 us
    pallas_call x1, Pallas kernels: 48.1 us -> 21.3 us  [local_vis(): pl.pallas_call(functools.partial(vis_kernel, nf, ns, chan_count), grid=(n...]
    unnamed x16 -> x8, local copies, waits for them, and re-layouts: 5.35 us -> 2.84 us
where the time goes in v2:
time: 38.3 us; the launch traced here: 38.1 us
  Pallas kernels  35.2 us (92%)
  local copies, waits for them, and re-layouts  2.84 us (7%)
    pallas_call x1, Pallas kernels, local_vis(): pl.pallas_call(functools.partial(vis_kernel, nf, ns, chan_count), grid=(n...  21.3 us
    pallas_call x1, Pallas kernels, exchange(): pl.pallas_call(functools.partial(exchange_kernel, nf, ns, scale), out_sha...  13.9 us
    unnamed x8, local copies, waits for them, and re-layouts  2.84 us

profile of v2, /device:TPU:0, one launch (start us, length us, event | category | flops | bytes accessed | tf_op | source)
XLA Modules:
  0.0 38.1 jit_solution(16611498674768055064)
XLA Ops:
  0.0 0.0 copy-start.1
  0.0 0.0 copy-start.2
  0.0 1.3 %copy.10.dir_ref = f32[1,3,128]{2,1,0:T(4,128)} copy(f32[1,3,128]{2,0,1:T(1,128)} %param.10) | data formatting | bytes 3072 | tf_op args[1]
  1.3 21.3 %shard_map.91.w_ref = bf16[8,64,256]{2,1,0:T(8,128)(2,1)} custom-call(bf16[1,128,8,32,128]{4,3,2,1,0:T(8,128)(2,1)} %jones_ref.1, f32[1,3,128]{2,1,0:T(4,128)} %copy.10.dir_ref, f32[1,128]{1,0:T(1,128)} %bitcast.9, f32[1,128]{1,0:T(1,128)} %bitcast.10, f32[3,128]{1,0:T(4,128)} %ant_ref.1, s32[1,512]{1,0:T(1,128)} %visible_ref.1, s32[2,256]{1,0:T(2,128)} %pairs_ref.1, ...), custom_call_target="tpu_custom_call" | custom-call | tf_op jit(solution)/shard_map/pallas_call | solution.py:179
  22.6 0.0 copy-done.1
  22.6 0.0 copy-done.2
  22.6 0.0 copy-start
  22.6 0.9 %copy-done = bf16[8,64,256]{2,1,0:T(8,128)(2,1)S(1)} copy-done((bf16[8,64,256]{2,1,0:T(8,128)(2,1)S(1)}, bf16[8,64,256]{2,1,0:T(8,128)(2,1)}, u32[]{:S(2)}) %copy-start) | copy-done | bytes 262168
  23.5 13.9 %shard_map.92 = f32[8,128]{1,0:T(8,128)S(1)} custom-call(bf16[8,64,256]{2,1,0:T(8,128)(2,1)S(1)} %copy-done, f32[128,256]{1,0:T(8,128)S(1)} %copy-done.1, s32[1,256]{1,0:T(1,128)S(1)} %bitcast.8), custom_call_target="tpu_custom_call" | custom-call | tf_op jit(solution)/shard_map/pallas_call | solution.py:290
  37.5 0.6 %copy.13 = f32[2,1,4,128]{3,2,1,0:T(4,128)} copy(f32[2,1,4,128]{3,2,1,0:T(4,128)S(1)} %bitcast.6) | data formatting | bytes 8192
Async XLA Ops:
  0.0 22.6 %copy-start.1 = (f32[128,256]{1,0:T(8,128)S(1)}, f32[128,256]{1,0:T(8,128)}, u32[]{:S(2)}) copy-start(f32[128,256]{1,0:T(8,128)} %constant.2.clone.table_ref) | copy-start | bytes 393220
  0.0 22.6 %copy-start.2 = (s32[256]{0:T(256)S(1)}, s32[256]{0:T(256)}, u32[]{:S(2)}) copy-start(s32[256]{0:T(256)} %param.16) | copy-start | bytes 3076
  22.6 1.0 %copy-start = (bf16[8,64,256]{2,1,0:T(8,128)(2,1)S(1)}, bf16[8,64,256]{2,1,0:T(8,128)(2,1)}, u32[]{:S(2)}) copy-start(bf16[8,64,256]{2,1,0:T(8,128)(2,1)} %shard_map.91.w_ref) | copy-start | bytes 786436

commit v3 on v2

v3 whole, which is shorter than its diff:
```python
import functools
import math

import jax
import jax.numpy as jnp
import numpy as np
from jax import lax
from jax.experimental import pallas as pl
from jax.experimental.pallas import tpu as pltpu
from jax.sharding import PartitionSpec as P

GD = 2
SLOTS = 16
SPEED_LIGHT = 299792458.0
START_FREQ = 100000000.0
BAND_WIDTH = 100000000.0
PIVOT_FREQ = 150000000.0
HIGHEST = lax.Precision.HIGHEST
F32 = jnp.float32
BF16 = jnp.bfloat16
MESH = pl.DeviceIdType.MESH
ABLK = 16
KC = 16
PAD = 8

SIN_C = [(-1.0) ** i / math.factorial(2 * i + 1) for i in range(6)]
COS_C = [(-1.0) ** i / math.factorial(2 * i) for i in range(7)]


def dot_t(a, b):
    return lax.dot_general(a, b, (((1,), (1,)), ((), ())), preferred_element_type=F32)


def cos_sin_turns(x):
    r = x - jnp.round(x)
    h = r * math.pi
    h2 = h * h
    s = SIN_C[-1]
    for c in SIN_C[-2::-1]:
        s = s * h2 + c
    s = s * h
    c_ = COS_C[-1]
    for c in COS_C[-2::-1]:
        c_ = c_ * h2 + c
    s2 = s + s
    return 1.0 - s2 * s, s2 * c_


def kernel(
    nf, ns, chan_count, scale,
    jones_ref, dir_ref, bright_ref, spec_ref, ant_ref, visible_ref, pairs_ref, group_ref,
    table_ref, out_ref,
    zbuf, geo_ref, stepc_ref, steps_ref, amp_ref, oa_ref, ob_ref, hit_ref, vbuf,
    wbuf, rbuf, sbuf, dbuf, send1, recv1, send2, recv2,
):
    step = pl.program_id(0)
    steps = pl.num_programs(0)
    na = ant_ref.shape[1]
    kd = jones_ref.shape[3]
    sd = jones_ref.shape[4]
    nbl = pairs_ref.shape[1]
    vis_total = visible_ref.shape[1]
    per = nf * SLOTS
    df = BAND_WIDTH / chan_count
    f = lax.axis_index("freq")
    j = lax.axis_index("src")
    chan_base = f * kd
    barrier = pltpu.get_barrier_semaphore()

    @pl.when(step == 0)
    def _():
        for o in range(1, ns):
            pl.semaphore_signal(
                barrier, inc=1, device_id=(f, lax.rem(j + o, ns)), device_id_type=MESH
            )
        for o in range(1, nf):
            pl.semaphore_signal(
                barrier, inc=1, device_id=(lax.rem(f + o, nf), j), device_id_type=MESH
            )
        ants = jnp.transpose(
            jnp.concatenate([ant_ref[...], jnp.zeros((na - 3, na), F32)], axis=0)
        )
        dirs = dir_ref[0]
        geo = (
            ants[:, 0:1] * dirs[0:1, :]
            + ants[:, 1:2] * dirs[1:2, :]
            + ants[:, 2:3] * dirs[2:3, :]
        )
        geo_ref[...] = geo
        c8, s8 = cos_sin_turns(geo * (8.0 * df / SPEED_LIGHT))
        stepc_ref[...] = c8
        steps_ref[...] = s8
        at = lax.broadcasted_iota(jnp.int32, (sd, vis_total), 0) + j * sd
        hit = (at == visible_ref[...]).astype(F32).astype(BF16)
        weight = dot_t(jnp.ones((8, vis_total), BF16), hit)[0:1]
        chan = lax.broadcasted_iota(jnp.int32, (kd, sd), 0) + chan_base
        freq = START_FREQ + chan.astype(F32) * df
        amp_ref[...] = (
            jnp.sqrt(bright_ref[...] * jnp.exp(-spec_ref[...] * jnp.log(freq / PIVOT_FREQ)))
            * weight
        )
        ids = lax.broadcasted_iota(jnp.int32, (na, nbl), 0)
        oa_ref[...] = (ids == pairs_ref[0:1, :]).astype(F32).astype(BF16)
        ob_ref[...] = (ids == pairs_ref[1:2, :]).astype(F32)
        owner = group_ref[...] // GD
        mine = lax.broadcasted_iota(jnp.int32, (nf * ns, nbl), 0) == owner
        mine_f = mine.astype(F32)
        before = lax.broadcasted_iota(jnp.int32, (nbl, nbl), 0) < lax.broadcasted_iota(
            jnp.int32, (nbl, nbl), 1
        )
        counts = jnp.dot(
            mine_f.astype(BF16), before.astype(F32).astype(BF16), preferred_element_type=F32
        )
        rank = jnp.sum(counts * mine_f, axis=0, keepdims=True).astype(jnp.int32)
        slot = ((owner % ns) * nf + owner // ns) * SLOTS + rank
        for b in range(ns):
            place = lax.broadcasted_iota(jnp.int32, (per, nbl), 0) + b * per
            hit_ref[b] = (place == slot).astype(F32).astype(BF16)

    chan8 = lax.broadcasted_iota(jnp.int32, (8, sd), 0) + chan_base
    turn_rate = (START_FREQ + chan8.astype(F32) * df) * (1.0 / SPEED_LIGHT)

    def build(i, carry):
        a = step * ABLK + i
        c, s = cos_sin_turns(geo_ref[pl.ds(a, 1), :] * turn_rate)
        cd = stepc_ref[pl.ds(a, 1), :]
        sdl = steps_ref[pl.ds(a, 1), :]
        cs, ss = [c], [s]
        for _ in range(kd // 8 - 1):
            c, s = c * cd - s * sdl, s * cd + c * sdl
            cs.append(c)
            ss.append(s)
        amp = amp_ref[...]
        ca = jnp.concatenate(cs, axis=0) * amp
        sa = jnp.concatenate(ss, axis=0) * amp
        rows = pl.ds(pl.multiple_of(a * (kd + PAD), 8), kd)
        for pq in range(4):
            br = jones_ref[0, i, pq].astype(F32)
            bi = jones_ref[0, i, 4 + pq].astype(F32)
            zbuf[pq, rows, :] = br * ca + bi * sa
            zbuf[4 + pq, rows, :] = bi * ca - br * sa
        return carry

    lax.fori_loop(0, ABLK, build, 0, unroll=4)

    @pl.when(step == steps - 1)
    def _():
        def channel(h, k, carry):
            def z(r, p, q):
                return zbuf[
                    4 * r + 2 * p + q, pl.ds(h * KC + k, na, stride=kd + PAD), :
                ].astype(BF16)

            zr = jnp.concatenate(
                [jnp.concatenate([z(0, p, 0), z(0, p, 1)], axis=1) for p in range(2)], axis=0
            )
            zi = jnp.concatenate(
                [jnp.concatenate([z(1, p, 0), z(1, p, 1)], axis=1) for p in range(2)], axis=0
            )
            left = jnp.concatenate([zr, zi], axis=1)
            turned = jnp.concatenate([zi, -zr], axis=1)
            oa = oa_ref[...]
            ob = ob_ref[...]
            rows = []
            for right in (left, turned):
                gram = dot_t(left, right).astype(BF16)
                for p in range(2):
                    picked = jnp.dot(
                        gram[:, p * na : (p + 1) * na], oa, preferred_element_type=F32
                    )
                    for p2 in range(2):
                        rows.append(
                            jnp.sum(
                                picked[p2 * na : (p2 + 1) * na] * ob, axis=0, keepdims=True
                            )
                        )
            vis = jnp.concatenate(rows, axis=0)
            for t in range(nbl // 128):
                vbuf[t, pl.ds(k, 8, stride=KC), :] = vis[:, t * 128 : (t + 1) * 128]
            return carry

        chunks = kd // KC
        first = [[] for _ in range(chunks)]
        second = [[] for _ in range(chunks)]

        def send_src(h):
            for o in range(1, ns):
                to = lax.rem(j + o, ns)
                copy = pltpu.make_async_remote_copy(
                    src_ref=wbuf.at[h, to],
                    dst_ref=rbuf.at[h, o - 1],
                    send_sem=send1.at[h, o - 1],
                    recv_sem=recv1.at[h, o - 1],
                    device_id=(f, to),
                    device_id_type=MESH,
                )
                copy.start()
                first[h].append(copy)

        def send_freq(h):
            total = wbuf[h, j].astype(F32)
            for o in range(1, ns):
                first[h][o - 1].wait_recv()
                total = total + rbuf[h, o - 1].astype(F32)
            sbuf[h] = total.reshape(nf, SLOTS, 8 * KC)
            for o in range(1, nf):
                to = lax.rem(f + o, nf)
                copy = pltpu.make_async_remote_copy(
                    src_ref=sbuf.at[h, to],
                    dst_ref=dbuf.at[h, f],
                    send_sem=send2.at[h, o - 1],
                    recv_sem=recv2.at[h, o - 1],
                    device_id=(to, j),
                    device_id_type=MESH,
                )
                copy.start()
                second[h].append(copy)
            dbuf[h, f] = sbuf[h, f]

        def transform(h):
            for copy in second[h]:
                copy.wait_recv()
            blocks = [dbuf[h, i] for i in range(nf)]
            vis = jnp.concatenate(
                [
                    jnp.concatenate([b[:, c * KC : (c + 1) * KC] for b in blocks], axis=1)
                    for c in range(8)
                ],
                axis=0,
            )
            return jnp.dot(vis, table_ref[h], precision=HIGHEST, preferred_element_type=F32)

        for h in range(chunks):
            lax.fori_loop(0, KC, functools.partial(channel, h), 0, unroll=8)
            vals = jnp.concatenate([vbuf[t] for t in range(nbl // 128)], axis=1).astype(BF16)
            for b in range(ns):
                wbuf[h, b] = dot_t(hit_ref[b], vals).astype(BF16)
            if h == 0:
                pl.semaphore_wait(barrier, ns + nf - 2)
            send_src(h)
        dev = f * ns + j
        groups = group_ref[...]
        shape = (8, 4 * SLOTS)
        row = lax.broadcasted_iota(jnp.int32, shape, 0)
        col = lax.broadcasted_iota(jnp.int32, shape, 1)
        mean = jnp.zeros(shape, F32)
        start = jnp.zeros((1, 1), F32)
        slot = (col % SLOTS).astype(F32)
        for g in range(GD):
            count = jnp.sum((groups == dev * GD + g).astype(F32), axis=1, keepdims=True)
            inside = (row // 4 == g) & (row % 4 == col // SLOTS)
            inside = inside & (slot >= start) & (slot < start + count)
            mean = mean + jnp.where(inside, 1.0 / (count * scale), 0.0)
            start = start + count
        both = 0.0
        for h in range(chunks):
            send_freq(h)
            if h < chunks - 1:
                both = both + transform(h)
        both = both + transform(chunks - 1)
        nu = table_ref.shape[2] // 2
        half = 4 * SLOTS
        real = both[:half, :nu] + both[half:, nu:]
        imag = both[half:, :nu] - both[:half, nu:]
        power = real * real + imag * imag
        out_ref[...] = jnp.dot(mean, power, precision=HIGHEST, preferred_element_type=F32)
        for h in range(chunks):
            for copy in first[h] + second[h]:
                copy.wait_send()


def fused(nf, ns, chan_count, scale, jones, *small):
    na, kd, sd = jones.shape[1], jones.shape[3], jones.shape[4]
    nbl = small[5].shape[1]
    chunks = kd // KC
    per = nf * SLOTS
    whole = lambda x: pl.BlockSpec(x.shape, lambda i: (0,) * x.ndim)
    return pl.pallas_call(
        functools.partial(kernel, nf, ns, chan_count, scale),
        grid=(na // ABLK,),
        out_shape=jax.ShapeDtypeStruct((8, chan_count), F32),
        in_specs=[pl.BlockSpec((1, ABLK, 8, kd, sd), lambda i: (0, i, 0, 0, 0))]
        + [whole(x) for x in small],
        out_specs=pl.BlockSpec((8, chan_count), lambda i: (0, 0)),
        scratch_shapes=[
            pltpu.VMEM((8, na * (kd + PAD), sd), F32),
            pltpu.VMEM((na, sd), F32),
            pltpu.VMEM((na, sd), F32),
            pltpu.VMEM((na, sd), F32),
            pltpu.VMEM((kd, sd), F32),
            pltpu.VMEM((na, nbl), BF16),
            pltpu.VMEM((na, nbl), F32),
            pltpu.VMEM((ns, per, nbl), BF16),
            pltpu.VMEM((nbl // 128, 8 * KC, 128), F32),
            pltpu.VMEM((chunks, ns, per, 8 * KC), BF16),
            pltpu.VMEM((chunks, ns - 1, per, 8 * KC), BF16),
            pltpu.VMEM((chunks, nf, SLOTS, 8 * KC), F32),
            pltpu.VMEM((chunks, nf, SLOTS, 8 * KC), F32),
            pltpu.SemaphoreType.DMA((chunks, ns - 1)),
            pltpu.SemaphoreType.DMA((chunks, ns - 1)),
            pltpu.SemaphoreType.DMA((chunks, nf - 1)),
            pltpu.SemaphoreType.DMA((chunks, nf - 1)),
        ],
        compiler_params=pltpu.CompilerParams(
            collective_id=0, has_side_effects=True, vmem_limit_bytes=60 * 1024 * 1024
        ),
    )(jones, *small)


def delay_table(chan_count, nf):
    k = np.arange(chan_count)
    angles = 2.0 * np.pi * k / chan_count
    taper = (
        0.35875
        - 0.48829 * np.cos(angles)
        + 0.14128 * np.cos(2.0 * angles)
        - 0.01168 * np.cos(3.0 * angles)
    )
    phases = 2.0 * np.pi * ((k[:, None] * k[None, :]) % chan_count) / chan_count
    both = np.concatenate([np.cos(phases), np.sin(phases)], axis=1) * taper[:, None]
    both = both.reshape(nf, -1, KC, 2 * chan_count).transpose(1, 0, 2, 3)
    return both.reshape(-1, nf * KC, 2 * chan_count).astype(np.float32)


def per_device(nf, ns, jones, directions, brightness, spectral, antennas, visible, pairs, group_of):
    chan_count = jones.shape[3] * nf
    groups = group_of.reshape(1, -1)
    table = jnp.asarray(delay_table(chan_count, nf))
    out = fused(
        nf, ns, chan_count, float(visible.shape[1] * chan_count), jones, directions,
        brightness.reshape(1, -1), spectral.reshape(1, -1), antennas, visible, pairs, groups, table,
    )
    return out.reshape(GD, 1, 4, chan_count)


def solution(mesh):
    nf, ns = mesh.shape["freq"], mesh.shape["src"]
    return jax.shard_map(
        functools.partial(per_device, nf, ns),
        mesh=mesh,
        in_specs=(
            P(None, None, None, "freq", "src"),
            P(None, None, "src"),
            P("src"),
            P("src"),
            P(),
            P(),
            P(),
            P(),
        ),
        out_specs=P(("freq", "src"), None, None, None),
        check_vma=False,
    )
```

time: 38.3 us -> 36.3 us (0.948)
  Pallas kernels: 35.2 us -> 33.5 us
    pallas_call x2 -> x1, Pallas kernels: 35.2 us -> 33.5 us  [fused(): pl.pallas_call(functools.partial(kernel, nf, ns, chan_count, scale), grid...]
    unnamed x8 -> x2, local copies, waits for them, and re-layouts: 2.84 us -> 2.53 us
where the time goes in v3:
time: 36.3 us; the launch traced here: 36 us
  Pallas kernels  33.5 us (92%)
  local copies, waits for them, and re-layouts  2.53 us (7%)
    pallas_call x1, Pallas kernels, fused(): pl.pallas_call(functools.partial(kernel, nf, ns, chan_count, scale), grid...  33.5 us
    unnamed x2, local copies, waits for them, and re-layouts  2.53 us

profile of v3, /device:TPU:0, one launch (start us, length us, event | category | flops | bytes accessed | tf_op | source)
XLA Modules:
  0.0 36.0 jit_solution(18064190101929887152)
XLA Ops:
  0.0 1.3 %copy.10.dir_ref = f32[1,3,128]{2,1,0:T(4,128)} copy(f32[1,3,128]{2,0,1:T(1,128)} %param.10) | data formatting | bytes 3072 | tf_op args[1]
  1.3 33.5 %shard_map.91 = f32[8,128]{1,0:T(8,128)} custom-call(bf16[1,128,8,32,128]{4,3,2,1,0:T(8,128)(2,1)} %jones_ref.1, f32[1,3,128]{2,1,0:T(4,128)} %copy.10.dir_ref, f32[1,128]{1,0:T(1,128)} %bitcast.8, f32[1,128]{1,0:T(1,128)} %bitcast.9, f32[3,128]{1,0:T(4,128)} %ant_ref.1, s32[1,512]{1,0:T(1,128)} %visible_ref.1, s32[2,256]{1,0:T(2,128)} %pairs_ref.1, ...), custom_call_target="tpu_custom_call" | custom-call | tf_op jit(solution)/shard_map/pallas_call | solution.py:278
  34.7 1.3 %copy.13 = f32[2,1,4,128]{3,2,1,0:T(4,128)} copy(f32[2,1,4,128]{3,2,1,0:T(4,128)} %bitcast.6) | data formatting | bytes 8192

commit v4 on v3

v4 whole, which is shorter than its diff:
```python
import functools
import math

import jax
import jax.numpy as jnp
import numpy as np
from jax import lax
from jax.experimental import pallas as pl
from jax.experimental.pallas import tpu as pltpu
from jax.sharding import PartitionSpec as P

GD = 2
SLOTS = 16
SPEED_LIGHT = 299792458.0
START_FREQ = 100000000.0
BAND_WIDTH = 100000000.0
PIVOT_FREQ = 150000000.0
HIGHEST = lax.Precision.HIGHEST
F32 = jnp.float32
BF16 = jnp.bfloat16
MESH = pl.DeviceIdType.MESH
BLOCKS = 8
PARTS = 2
KC = 16
PAD = 8

SIN_C = [(-1.0) ** i / math.factorial(2 * i + 1) for i in range(6)]
COS_C = [(-1.0) ** i / math.factorial(2 * i) for i in range(7)]


def dot_t(a, b):
    return lax.dot_general(a, b, (((1,), (1,)), ((), ())), preferred_element_type=F32)


def cos_sin_turns(x):
    r = x - jnp.round(x)
    h = r * math.pi
    h2 = h * h
    s = SIN_C[-1]
    for c in SIN_C[-2::-1]:
        s = s * h2 + c
    s = s * h
    c_ = COS_C[-1]
    for c in COS_C[-2::-1]:
        c_ = c_ * h2 + c
    s2 = s + s
    return 1.0 - s2 * s, s2 * c_


def kernel(
    nf, ns, chan_count, scale,
    jones_ref, *refs,
):
    small_hbm, out_ref = refs[:8], refs[8]
    dir_ref, bright_ref, spec_ref, ant_ref, visible_ref, pairs_ref, group_ref, table_ref = refs[
        9:17
    ]
    (
        jbuf, geo_ref, stepc_ref, steps_ref, amp_ref, oa_ref, ob_ref, hit_ref, vbuf,
        wbuf, rbuf, sbuf, dbuf, small_sem, jones_sem, send1, recv1, send2, recv2,
    ) = refs[17:36]
    zbufs = refs[36:]
    na = ant_ref.shape[1]
    kd = jones_ref.shape[3]
    chunks = kd // KC
    sd = jones_ref.shape[4]
    nbl = pairs_ref.shape[1]
    vis_total = visible_ref.shape[1]
    per = nf * SLOTS
    df = BAND_WIDTH / chan_count
    f = lax.axis_index("freq")
    j = lax.axis_index("src")
    chan_base = f * kd
    barrier = pltpu.get_barrier_semaphore()

    for o in range(1, ns):
        pl.semaphore_signal(
            barrier, inc=1, device_id=(f, lax.rem(j + o, ns)), device_id_type=MESH
        )
    for o in range(1, nf):
        pl.semaphore_signal(
            barrier, inc=1, device_id=(lax.rem(f + o, nf), j), device_id_type=MESH
        )
    small_copies = [
        pltpu.make_async_copy(x, y, small_sem.at[i])
        for i, (x, y) in enumerate(zip(small_hbm, refs[9:17]))
    ]
    for copy in small_copies[:-1]:
        copy.start()
    ab = na // BLOCKS

    def beams(h, i):
        return pltpu.make_async_copy(
            jones_ref.at[0, pl.ds(i * ab, ab), :, pl.ds(h * KC, KC), :],
            jbuf.at[h, pl.ds(i * ab, ab)],
            jones_sem.at[h, i],
        )

    for h in range(chunks):
        for i in range(BLOCKS):
            beams(h, i).start()
    small_copies[-1].start()
    for copy in small_copies[:-1]:
        copy.wait()
    ants = jnp.transpose(
        jnp.concatenate([ant_ref[...], jnp.zeros((na - 3, na), F32)], axis=0)
    )
    dirs = [dir_ref[:, i * sd : (i + 1) * sd] for i in range(3)]
    geo = (
        ants[:, 0:1] * dirs[0]
        + ants[:, 1:2] * dirs[1]
        + ants[:, 2:3] * dirs[2]
    )
    geo_ref[...] = geo
    c8, s8 = cos_sin_turns(geo * (8.0 * df / SPEED_LIGHT))
    stepc_ref[...] = c8
    steps_ref[...] = s8
    at = lax.broadcasted_iota(jnp.int32, (sd, vis_total), 0) + j * sd
    hit = (at == visible_ref[...]).astype(F32).astype(BF16)
    weight = dot_t(jnp.ones((8, vis_total), BF16), hit)[0:1]
    chan = lax.broadcasted_iota(jnp.int32, (kd, sd), 0) + chan_base
    freq = START_FREQ + chan.astype(F32) * df
    amp_ref[...] = (
        jnp.sqrt(bright_ref[...] * jnp.exp(-spec_ref[...] * jnp.log(freq / PIVOT_FREQ)))
        * weight
    )
    ids = lax.broadcasted_iota(jnp.int32, (na, nbl), 0)
    oa_ref[...] = (ids == pairs_ref[0:1, :]).astype(F32).astype(BF16)
    ob_ref[...] = (ids == pairs_ref[1:2, :]).astype(F32)
    owner = group_ref[...] // GD
    mine = lax.broadcasted_iota(jnp.int32, (nf * ns, nbl), 0) == owner
    mine_f = mine.astype(F32)
    before = lax.broadcasted_iota(jnp.int32, (nbl, nbl), 0) < lax.broadcasted_iota(
        jnp.int32, (nbl, nbl), 1
    )
    counts = jnp.dot(
        mine_f.astype(BF16), before.astype(F32).astype(BF16), preferred_element_type=F32
    )
    rank = jnp.sum(counts * mine_f, axis=0, keepdims=True).astype(jnp.int32)
    slot = ((owner % ns) * nf + owner // ns) * SLOTS + rank
    for b in range(ns):
        place = lax.broadcasted_iota(jnp.int32, (per, nbl), 0) + b * per
        hit_ref[b] = (place == slot).astype(F32).astype(BF16)

    chan8 = lax.broadcasted_iota(jnp.int32, (8, sd), 0) + chan_base

    def build(h, a):
        rate = (START_FREQ + (chan8 + h * KC).astype(F32) * df) * (1.0 / SPEED_LIGHT)
        c, s = cos_sin_turns(geo_ref[pl.ds(a, 1), :] * rate)
        cd = stepc_ref[pl.ds(a, 1), :]
        sdl = steps_ref[pl.ds(a, 1), :]
        cs, ss = [c], [s]
        for _ in range(KC // 8 - 1):
            c, s = c * cd - s * sdl, s * cd + c * sdl
            cs.append(c)
            ss.append(s)
        amp = amp_ref[h * KC : (h + 1) * KC]
        ca = jnp.concatenate(cs, axis=0) * amp
        sa = jnp.concatenate(ss, axis=0) * amp
        rows = pl.ds(pl.multiple_of(a * (KC + PAD), 8), KC)
        for pq in range(4):
            br = jbuf[h, a, pq].astype(F32)
            bi = jbuf[h, a, 4 + pq].astype(F32)
            zbufs[h][pq, rows, :] = br * ca + bi * sa
            zbufs[h][4 + pq, rows, :] = bi * ca - br * sa

    def build_first(i, carry):
        build(0, i)
        return carry

    for i in range(BLOCKS):
        beams(0, i).wait()
        lax.fori_loop(i * ab, (i + 1) * ab, build_first, 0, unroll=8)

    def channel(h, k):
        def z(r, p, q):
            return zbufs[h][
                4 * r + 2 * p + q, pl.ds(k, na, stride=KC + PAD), :
            ].astype(BF16)

        zr = jnp.concatenate(
            [jnp.concatenate([z(0, p, 0), z(0, p, 1)], axis=1) for p in range(2)], axis=0
        )
        zi = jnp.concatenate(
            [jnp.concatenate([z(1, p, 0), z(1, p, 1)], axis=1) for p in range(2)], axis=0
        )
        left = jnp.concatenate([zr, zi], axis=1)
        both = jnp.concatenate([left, jnp.concatenate([-zi, zr], axis=1)], axis=0)
        gram = dot_t(both, left).astype(BF16)
        gram = jnp.concatenate([gram[:, :na], gram[:, na:]], axis=0)
        picked = jnp.dot(gram, oa_ref[...], preferred_element_type=F32)
        ob = ob_ref[...]
        rows = []
        for r in range(2):
            for p in range(2):
                for p2 in range(2):
                    at = ((p * 2 + r) * 2 + p2) * na
                    rows.append(
                        jnp.sum(picked[at : at + na] * ob, axis=0, keepdims=True)
                    )
        vis = jnp.concatenate(rows, axis=0)
        for t in range(nbl // 128):
            vbuf[t, pl.ds(k, 8, stride=KC), :] = vis[:, t * 128 : (t + 1) * 128]

    batch = KC // PARTS

    def channels(h, t, carry):
        if h + 1 < chunks:
            for i in range(BLOCKS // PARTS):
                beams(h + 1, t * (BLOCKS // PARTS) + i).wait()
        for u in range(batch):
            channel(h, t * batch + u)
            if h + 1 < chunks:
                for v in range(na // KC):
                    build(h + 1, (t * batch + u) * (na // KC) + v)
        return carry

    first = [[] for _ in range(chunks)]
    second = [[] for _ in range(chunks)]

    def send_src(h):
        for o in range(1, ns):
            to = lax.rem(j + o, ns)
            copy = pltpu.make_async_remote_copy(
                src_ref=wbuf.at[h, to],
                dst_ref=rbuf.at[h, o - 1],
                send_sem=send1.at[h, o - 1],
                recv_sem=recv1.at[h, o - 1],
                device_id=(f, to),
                device_id_type=MESH,
            )
            copy.start()
            first[h].append(copy)

    def send_freq(h):
        total = wbuf[h, j].astype(F32)
        for o in range(1, ns):
            first[h][o - 1].wait_recv()
            total = total + rbuf[h, o - 1].astype(F32)
        sbuf[h] = total.reshape(nf, SLOTS, 8 * KC)
        for o in range(1, nf):
            to = lax.rem(f + o, nf)
            copy = pltpu.make_async_remote_copy(
                src_ref=sbuf.at[h, to],
                dst_ref=dbuf.at[h, f],
                send_sem=send2.at[h, o - 1],
                recv_sem=recv2.at[h, o - 1],
                device_id=(to, j),
                device_id_type=MESH,
            )
            copy.start()
            second[h].append(copy)
        dbuf[h, f] = sbuf[h, f]

    def transform(h):
        for copy in second[h]:
            copy.wait_recv()
        blocks = [dbuf[h, i] for i in range(nf)]
        vis = jnp.concatenate(
            [
                jnp.concatenate([b[:, c * KC : (c + 1) * KC] for b in blocks], axis=1)
                for c in range(8)
            ],
            axis=0,
        )
        return jnp.dot(vis, table_ref[h], precision=HIGHEST, preferred_element_type=F32)

    for h in range(chunks):
        lax.fori_loop(0, PARTS, functools.partial(channels, h), 0)
        vals = jnp.concatenate([vbuf[t] for t in range(nbl // 128)], axis=1).astype(BF16)
        for b in range(ns):
            wbuf[h, b] = dot_t(hit_ref[b], vals).astype(BF16)
        if h == 0:
            pl.semaphore_wait(barrier, ns + nf - 2)
        send_src(h)
    dev = f * ns + j
    groups = group_ref[...]
    shape = (8, 4 * SLOTS)
    row = lax.broadcasted_iota(jnp.int32, shape, 0)
    col = lax.broadcasted_iota(jnp.int32, shape, 1)
    mean = jnp.zeros(shape, F32)
    start = jnp.zeros((1, 1), F32)
    slot = (col % SLOTS).astype(F32)
    for g in range(GD):
        count = jnp.sum((groups == dev * GD + g).astype(F32), axis=1, keepdims=True)
        inside = (row // 4 == g) & (row % 4 == col // SLOTS)
        inside = inside & (slot >= start) & (slot < start + count)
        mean = mean + jnp.where(inside, 1.0 / (count * scale), 0.0)
        start = start + count
    small_copies[-1].wait()
    both = 0.0
    for h in range(chunks):
        send_freq(h)
        if h < chunks - 1:
            both = both + transform(h)
    both = both + transform(chunks - 1)
    nu = table_ref.shape[2] // 2
    half = 4 * SLOTS
    real = both[:half, :nu] + both[half:, nu:]
    imag = both[half:, :nu] - both[:half, nu:]
    power = real * real + imag * imag
    out_ref[...] = jnp.dot(mean, power, precision=HIGHEST, preferred_element_type=F32)
    for h in range(chunks):
        for copy in first[h] + second[h]:
            copy.wait_send()


def fused(nf, ns, chan_count, scale, jones, *small):
    na, kd, sd = jones.shape[1], jones.shape[3], jones.shape[4]
    nbl = small[5].shape[1]
    chunks = kd // KC
    per = nf * SLOTS
    return pl.pallas_call(
        functools.partial(kernel, nf, ns, chan_count, scale),
        grid=(1,),
        out_shape=jax.ShapeDtypeStruct((8, chan_count), F32),
        in_specs=[pl.BlockSpec(memory_space=pl.ANY)] * (1 + len(small)),
        out_specs=pl.BlockSpec((8, chan_count), lambda i: (0, 0)),
        scratch_shapes=[pltpu.VMEM(x.shape, x.dtype) for x in small]
        + [
            pltpu.VMEM((chunks, na, 8, KC, sd), BF16),
            pltpu.VMEM((na, sd), F32),
            pltpu.VMEM((na, sd), F32),
            pltpu.VMEM((na, sd), F32),
            pltpu.VMEM((kd, sd), F32),
            pltpu.VMEM((na, nbl), BF16),
            pltpu.VMEM((na, nbl), F32),
            pltpu.VMEM((ns, per, nbl), BF16),
            pltpu.VMEM((nbl // 128, 8 * KC, 128), F32),
            pltpu.VMEM((chunks, ns, per, 8 * KC), BF16),
            pltpu.VMEM((chunks, ns - 1, per, 8 * KC), BF16),
            pltpu.VMEM((chunks, nf, SLOTS, 8 * KC), F32),
            pltpu.VMEM((chunks, nf, SLOTS, 8 * KC), F32),
            pltpu.SemaphoreType.DMA((len(small),)),
            pltpu.SemaphoreType.DMA((chunks, BLOCKS)),
            pltpu.SemaphoreType.DMA((chunks, ns - 1)),
            pltpu.SemaphoreType.DMA((chunks, ns - 1)),
            pltpu.SemaphoreType.DMA((chunks, nf - 1)),
            pltpu.SemaphoreType.DMA((chunks, nf - 1)),
        ]
        + [pltpu.VMEM((8, na * (KC + PAD), sd), F32)] * chunks,
        compiler_params=pltpu.CompilerParams(
            collective_id=0, has_side_effects=True, vmem_limit_bytes=60 * 1024 * 1024
        ),
    )(jones, *small)


def delay_table(chan_count, nf):
    k = np.arange(chan_count)
    angles = 2.0 * np.pi * k / chan_count
    taper = (
        0.35875
        - 0.48829 * np.cos(angles)
        + 0.14128 * np.cos(2.0 * angles)
        - 0.01168 * np.cos(3.0 * angles)
    )
    phases = 2.0 * np.pi * ((k[:, None] * k[None, :]) % chan_count) / chan_count
    both = np.concatenate([np.cos(phases), np.sin(phases)], axis=1) * taper[:, None]
    both = both.reshape(nf, -1, KC, 2 * chan_count).transpose(1, 0, 2, 3)
    return both.reshape(-1, nf * KC, 2 * chan_count).astype(np.float32)


def per_device(nf, ns, jones, directions, brightness, spectral, antennas, visible, pairs, group_of):
    chan_count = jones.shape[3] * nf
    groups = group_of.reshape(1, -1)
    table = jnp.asarray(delay_table(chan_count, nf))
    out = fused(
        nf, ns, chan_count, float(visible.shape[1] * chan_count), jones, directions.reshape(1, -1),
        brightness.reshape(1, -1), spectral.reshape(1, -1), antennas, visible, pairs, groups, table,
    )
    return out.reshape(GD, 1, 4, chan_count)


def solution(mesh):
    nf, ns = mesh.shape["freq"], mesh.shape["src"]
    return jax.shard_map(
        functools.partial(per_device, nf, ns),
        mesh=mesh,
        in_specs=(
            P(None, None, None, "freq", "src"),
            P(None, None, "src"),
            P("src"),
            P("src"),
            P(),
            P(),
            P(),
            P(),
        ),
        out_specs=P(("freq", "src"), None, None, None),
        check_vma=False,
    )
```

time: 36.3 us -> 34.1 us (0.939)
  local copies, waits for them, and re-layouts: 2.53 us -> 1.28 us
  Pallas kernels: 33.5 us -> 32.6 us
    unnamed x2 -> x1, local copies, waits for them, and re-layouts: 2.53 us -> 1.28 us
    pallas_call x1, Pallas kernels: 33.5 us -> 32.6 us  [fused(): pl.pallas_call(functools.partial(kernel, nf, ns, chan_count, scale), grid...]
where the time goes in v4:
time: 34.1 us; the launch traced here: 33.9 us
  Pallas kernels  32.6 us (96%)
  local copies, waits for them, and re-layouts  1.28 us (4%)
    pallas_call x1, Pallas kernels, fused(): pl.pallas_call(functools.partial(kernel, nf, ns, chan_count, scale), grid...  32.6 us
    unnamed x1, local copies, waits for them, and re-layouts  1.28 us

profile of v4, /device:TPU:0, one launch (start us, length us, event | category | flops | bytes accessed | tf_op | source)
XLA Modules:
  0.0 33.9 jit_solution(16840332356242905025)
XLA Ops:
  0.0 32.6 %shard_map.91 = f32[8,128]{1,0:T(8,128)} custom-call(bf16[1,128,8,32,128]{4,3,2,1,0:T(8,128)(2,1)} %jones_ref.1, f32[1,384]{1,0:T(1,128)} %bitcast.8, f32[1,128]{1,0:T(1,128)} %bitcast.10, f32[1,128]{1,0:T(1,128)} %bitcast.11, f32[3,128]{1,0:T(4,128)} %refs_3_.1, s32[1,512]{1,0:T(1,128)} %refs_4_.1, s32[2,256]{1,0:T(2,128)} %refs_5_.1, s32[1,256]{1,0:T(1,128)} %bitcast.9, ...), custom_call_target="tpu_custom_call" | custom-call | tf_op jit(solution)/shard_map/pallas_call | solution.py:313
  32.6 1.3 %copy.12 = f32[2,1,4,128]{3,2,1,0:T(4,128)} copy(f32[2,1,4,128]{3,2,1,0:T(4,128)} %bitcast.7) | data formatting | bytes 8192
